TPU v7x, 32 devices: a whole 2x2x4 slice. The times are simulated.
32 devices in a mesh: rows: 8 (over z, x), cols: 4 (over y, core).
Axes of the slice: x: 2, y: 2, z: 4, core: 2. Of those that a mesh axis runs over, the one named last changes fastest.
Arguments:
- column_lists: int32 [32, 13], replicated, may hold values from -1 to 31, as said below
- block_values: bfloat16 [32, 13, 128, 128], P('rows'), as said below
Outputs:
- purified: bfloat16 [32, 13, 128, 128], P('rows', None, None, 'cols')
Inputs may be any that keep to these rules, and one draw needn't show every extreme that they name: `column_lists`: slot (13 - 1) // 2 of row i holds i. Slot s of row i holds -1 or a row j, and then slot 12 - s of row j holds i. There is an ordering of the rows, taken cyclically, in which the row in slot s of row i stands s - (13 - 1) // 2 places after row i. With owners the aligned groups of 4 rows, the slots of one owner's rows hold at most 2 rows of any one other owner, and some pair of owners has exactly 2. Over the slots s of one owner's rows that hold rows of one other owner, the sum of 13 - |s - (13 - 1) // 2| is at most 16, and exactly 16 for some pair of owners. block_values[j, 12 - s] is the transpose of block_values[i, s] where slot s of row i holds j; blocks of empty slots are zero.
All inputs are finite; a program needn't handle non-finite values.
Results may differ from a plain program's by a relative error of at most 0.0039.
Values may be sent and summed in bfloat16 or wider, within the bound.
A program may use at most 128 MiB of HBM per device.

v0:
```python
import jax
import jax.numpy as jnp
from jax import lax
from jax.sharding import PartitionSpec as P

CAP = 2


def body(column_lists, block_values):
    rows_here = block_values.shape[0]
    slot_count = block_values.shape[1]
    block_size = block_values.shape[2]
    middle = (slot_count - 1) // 2
    owners = lax.axis_size("rows")
    strip_width = block_size // lax.axis_size("cols")
    row_index = lax.axis_index("rows")
    column_part = lax.axis_index("cols")
    all_rows = column_lists.shape[0]
    present = column_lists >= 0
    target = jnp.maximum(column_lists, 0)
    owner_of = target // rows_here
    home_owner = (jnp.arange(all_rows, dtype=jnp.int32) // rows_here)[:, None]
    crossing = present & (owner_of != home_owner)
    dest_hot = (
        crossing[:, :, None] & (owner_of[:, :, None] == jnp.arange(owners, dtype=jnp.int32))
    ).astype(jnp.int32)
    first_row = row_index * rows_here
    own_present = lax.dynamic_slice_in_dim(present, first_row, rows_here, 0)
    my_cross = lax.dynamic_slice_in_dim(crossing, first_row, rows_here, 0)
    my_owner = lax.dynamic_slice_in_dim(owner_of, first_row, rows_here, 0)
    my_target = lax.dynamic_slice_in_dim(target, first_row, rows_here, 0)
    full_rows = jnp.where(
        own_present[:, :, None, None], block_values, jnp.zeros((), block_values.dtype)
    )
    own_strip = lax.dynamic_slice_in_dim(full_rows, column_part * strip_width, strip_width, 3)
    slot_ids = jnp.arange(slot_count, dtype=jnp.int32)
    running = jnp.cumsum(dest_hot.reshape(owners, rows_here * slot_count, owners), axis=1)
    running = running.reshape(all_rows, slot_count, owners)
    ranking = jnp.sum(running * dest_hot, axis=2) - 1
    my_rank = lax.dynamic_slice_in_dim(ranking, first_row, rows_here, 0)
    filler = jnp.zeros((1, slot_count - 1, block_size, strip_width), own_strip.dtype)
    local_stack = jnp.concatenate([own_strip[:, : slot_count - 1], own_strip[:, 1:], filler], 0)
    zero_entry = 2 * rows_here
    slot_of = jnp.where(my_cross, my_owner * CAP + my_rank, owners * CAP)
    stack_entry = (
        jnp.arange(rows_here, dtype=jnp.int32)[:, None]
        + jnp.where(slot_ids < middle, 0, rows_here)[None, :]
    )
    source = jnp.full((owners * CAP + 1,), zero_entry, jnp.int32)
    source = source.at[slot_of.reshape(-1)].set(stack_entry.reshape(-1))[: owners * CAP]
    outgoing = local_stack[source]
    back_rank = ranking[my_target, (slot_count - 1 - slot_ids)[None, :]]
    local_pick = (
        owners * CAP + my_target - first_row + jnp.where(slot_ids > middle, 0, rows_here)[None, :]
    )
    remote_pick = my_owner * CAP + back_rank
    empty_entry = owners * CAP + zero_entry
    table_pick = jnp.where(
        own_present & (my_owner == row_index),
        local_pick,
        jnp.where(own_present, remote_pick, empty_entry),
    )
    table_pick = table_pick.at[:, middle].set(empty_entry)
    arrived = lax.all_to_all(outgoing, "rows", split_axis=0, concat_axis=0, tiled=True)
    lookup = jnp.concatenate([arrived, local_stack], 0)
    picked = lookup[table_pick]
    by_slot = []
    for slot_index in range(slot_count):
        offset = slot_index - middle
        if offset == 0:
            by_slot.append(own_strip)
        elif offset > 0:
            by_slot.append(
                jnp.pad(
                    picked[:, slot_index, : slot_count - offset],
                    ((0, 0), (offset, 0), (0, 0), (0, 0)),
                )
            )
        else:
            by_slot.append(
                jnp.pad(
                    picked[:, slot_index, -offset - 1 :], ((0, 0), (0, -offset), (0, 0), (0, 0))
                )
            )
    windows = jnp.stack(by_slot, 1)
    square_sum = jnp.einsum(
        "iapq,iasqc->ispc", full_rows, windows, preferred_element_type=jnp.float32
    )
    square = jnp.where(own_present[:, :, None, None], square_sum, 0.0).astype(jnp.bfloat16)
    cube_sum = jnp.einsum(
        "iapq,iasqc->ispc",
        lax.all_gather(square, "cols", axis=3, tiled=True),
        windows,
        preferred_element_type=jnp.float32,
    )
    purified = jnp.where(
        own_present[:, :, None, None], 3.0 * square.astype(jnp.float32) - 2.0 * cube_sum, 0.0
    )
    return purified.astype(jnp.bfloat16)


def solution(mesh):
    in_specs = (P(), P("rows", None, None, None))
    out_specs = P("rows", None, None, "cols")
    return jax.shard_map(body, mesh=mesh, in_specs=in_specs, out_specs=out_specs, check_vma=False)
```

profile of v0, /device:TPU:1, one launch (start us, length us, event | category | flops | bytes accessed | tf_op | source)
XLA Modules:
  0.0 112.8 jit_solution(974837170081073199)
XLA Ops:
  6.7 0.8 copy.73
  8.0 1.2 %fusion.49 = s32[8,52]{0,1:T(8,128)S(1)} fusion(s32[8,52]{0,1:T(8,128)S(1)} %copy.77, pred[8,52]{0,1:T(8,128)(4,1)S(1)} %copy.76), kind=kOutput, calls=%fused_computation.95 | output fusion | flops 192608 | bytes 3744 | tf_op jit(solution)/shard_map/jit(cumsum)/reduce_window_sum | solution.py:37
  9.3 1.0 gather_fusion.1
  10.5 0.7 scatter_custom_fusion
  11.3 2.8 %copy.74 = bf16[4,13,128,128]{2,3,1,0:T(8,128)(2,1)S(1)} copy(bf16[4,13,128,128]{3,2,1,0:T(8,128)(2,1)} %param.5) | data formatting | bytes 3407872 | tf_op args[1]
  14.4 0.9 copy-done
  15.9 1.9 %gather_fusion = bf16[16,12,128,32]{2,3,1,0:T(8,128)(2,1)} fusion(bf16[9,12,128,32]{2,3,1,0:T(8,128)(2,1)S(1)} %pad_maximum_fusion.1, s32[1024]{0:T(1024)S(1)} %pad_clamp_fusion.1), kind=kCustom, calls=%fused_computation | custom fusion | bytes 3145792 | tf_op jit(solution)/shard_map/gather | solution.py:51
  17.9 6.4 %all-to-all-start = ((bf16[16,12,128,32]{2,3,1,0:T(8,128)(2,1)}), bf16[16,12,128,32]{2,3,1,0:T(8,128)(2,1)}, u32[]{:S(2)}, u32[]{:S(2)}) async-start(bf16[16,12,128,32]{2,3,1,0:T(8,128)(2,1)} %gather_fusion), calls=%async_computation | async-start | bytes 3145728 | tf_op jit(solution)/shard_map/all_to_all | solution.py:64
  24.3 0.6 compare_reduce_fusion
  24.9 0.7 slice_select_fusion
  25.8 34.6 %all-to-all-done = bf16[16,12,128,32]{2,3,1,0:T(8,128)(2,1)} async-done(((bf16[16,12,128,32]{2,3,1,0:T(8,128)(2,1)}), bf16[16,12,128,32]{2,3,1,0:T(8,128)(2,1)}, u32[]{:S(2)}, u32[]{:S(2)}) %all-to-all-start) | async-done | bytes 1572896 | tf_op jit(solution)/shard_map/all_to_all | solution.py:64
  60.5 1.6 %pad_maximum_fusion = bf16[25,12,128,32]{2,3,1,0:T(8,128)(2,1)S(1)} fusion(bf16[1,12,128,32]{2,3,1,0:T(8,128)(2,1)S(1)} %broadcast_in_dim.82, bf16[4,12,128,32]{2,3,1,0:T(8,128)(2,1)S(1)} %get-tuple-element.34, bf16[4,12,128,32]{2,3,1,0:T(8,128)(2,1)S(1)} %get-tuple-element.33, bf16[16,12,128,32]{2,3,1,0:T(8,128)(2,1)} %all-to-all-done), kind=kLoop, calls=%fused_computation.4 | loop fusion | flops 3686400 | bytes 4915200 | tf_op jit(solution)/shard_map/concatenate | solution.py:65
  62.1 3.6 %gather_fusion.2 = bf16[52,12,128,32]{2,3,1,0:T(8,128)(2,1)} fusion(bf16[25,12,128,32]{2,3,1,0:T(8,128)(2,1)S(1)} %pad_maximum_fusion, s32[1024]{0:T(1024)S(1)} %pad_clamp_fusion), kind=kCustom, calls=%fused_computation.2 | custom fusion | bytes 10223824 | tf_op jit(solution)/shard_map/gather | solution.py:66
  65.6 1.1 slice_bitcast_fusion.10
  66.7 1.1 slice_bitcast_fusion.8
  67.8 1.1 slice_bitcast_fusion.6
  68.9 1.1 slice_bitcast_fusion.4
  70.0 1.1 %slice_bitcast_fusion.2 = (bf16[4,11,128,32]{2,3,1,0:T(8,128)(2,1)S(1)}, bf16[4,11,128,32]{2,3,1,0:T(8,128)(2,1)S(1)}) fusion(bf16[4,13,12,128,32]{3,4,2,1,0:T(8,128)(2,1)} %bitcast.152), kind=kLoop, calls=%fused_computation.37 | loop fusion | bytes 1441792 | tf_op jit(solution)/shard_map/squeeze | solution.py:75
  71.2 1.3 %slice_bitcast_fusion = (bf16[4,12,128,32]{2,3,1,0:T(8,128)(2,1)S(1)}, bf16[4,12,128,32]{2,3,1,0:T(8,128)(2,1)S(1)}) fusion(bf16[4,13,12,128,32]{3,4,2,1,0:T(8,128)(2,1)} %bitcast.153), kind=kLoop, calls=%fused_computation.35 | loop fusion | bytes 1572864 | tf_op jit(solution)/shard_map/squeeze | solution.py:75
  72.9 1.1 bitcast_dynamic-update-slice_fusion.6
  74.5 2.4 %copy-done.3 = bf16[4,13,13,128,32]{3,4,1,2,0:T(8,128)(2,1)} copy-done((bf16[4,13,13,128,32]{3,4,1,2,0:T(8,128)(2,1)}, bf16[4,13,13,128,32]{3,4,1,2,0:T(8,128)(2,1)S(1)}, u32[]{:S(2)}) %copy-start.3) | copy-done | bytes 5537816
  76.9 2.4 %fusion.31 = bf16[4,13,128,32]{2,3,1,0:T(8,128)(2,1)} fusion(bf16[4,13,13,128,32]{3,4,1,2,0:T(8,128)(2,1)S(1)} %bitcast_dynamic-update-slice_fusion, pred[4,13]{1,0:T(4,128)(4,1)S(1)} %get-tuple-element.18, bf16[4,13,128,128]{2,3,1,0:T(8,128)(2,1)S(1)} %copy-done.1), kind=kOutput, calls=%fused_computation.19 | convolution fusion | flops 710115328 | bytes 7667764 | tf_op jit(solution)/shard_map/iapq,iasqc->ispc/dot_general | solution.py:86
  79.3 21.2 %all-gather.2.cloned.1.call-done = bf16[4,13,128,128]{2,3,1,0:T(8,128)(2,1)} async-done(((bf16[4,13,128,32]{2,3,1,0:T(8,128)(2,1)}), bf16[4,13,128,128]{2,3,1,0:T(8,128)(2,1)}) %all-gather.2.cloned.1.call-update) | async-done | bytes 1703952 | tf_op jit(solution)/shard_map/all_gather | solution.py:92
  100.5 5.4 %fusion.22 = bf16[4,13,128,32]{2,3,1,0:T(8,128)(2,1)} fusion(bf16[4,13,13,128,32]{3,4,1,2,0:T(8,128)(2,1)} %copy-done.3, bf16[4,13,128,128]{2,3,1,0:T(8,128)(2,1)} %all-gather.2.cloned.1.call-done, bf16[4,13,128,32]{2,3,1,0:T(8,128)(2,1)} %fusion.31, pred[4,13]{1,0:T(4,128)(4,1)S(1)} %get-tuple-element.18), kind=kOutput, calls=%fused_computation.16 | convolution fusion | flops 710115328 | bytes 8093748 | tf_op jit(solution)/shard_map/iapq,iasqc->ispc/dot_general | solution.py:90
  (50 shorter events, 3.0 us)
Async XLA Ops:
  14.1 1.2 %copy-start = (bf16[4,13,128,128]{2,3,1,0:T(8,128)(2,1)}, bf16[4,13,128,128]{2,3,1,0:T(8,128)(2,1)S(1)}, u32[]{:S(2)}) copy-start(bf16[4,13,128,128]{2,3,1,0:T(8,128)(2,1)S(1)} %copy.74) | copy-start | bytes 5111812
  14.3 1.5 %copy-start.2 = (bf16[4,13,128,128]{2,3,1,0:T(8,128)(2,1)}, bf16[4,13,128,128]{2,3,1,0:T(8,128)(2,1)S(1)}, u32[]{:S(2)}) copy-start(bf16[4,13,128,128]{2,3,1,0:T(8,128)(2,1)S(1)} %broadcast_select_fusion) | copy-start | bytes 5111812
  17.9 42.6 %all-to-all-start = ((bf16[16,12,128,32]{2,3,1,0:T(8,128)(2,1)}), bf16[16,12,128,32]{2,3,1,0:T(8,128)(2,1)}, u32[]{:S(2)}, u32[]{:S(2)}) async-start(bf16[16,12,128,32]{2,3,1,0:T(8,128)(2,1)} %gather_fusion), calls=%async_computation | async-start | bytes 3145728 | tf_op jit(solution)/shard_map/all_to_all | solution.py:64
  24.2 76.3 %all-gather.2.cloned.1.call-start = ((), (), s32[]{:S(2)}) async-start(), calls=%async_computation.1 | async-start | bytes 2129920 | tf_op jit(solution)/shard_map/all_gather | solution.py:92
  71.2 5.7 %copy-start.1 = (bf16[4,13,128,128]{2,3,1,0:T(8,128)(2,1)S(1)}, bf16[4,13,128,128]{2,3,1,0:T(8,128)(2,1)}, u32[]{:S(2)}) copy-start(bf16[4,13,128,128]{2,3,1,0:T(8,128)(2,1)} %copy-done) | copy-start | bytes 5111812
  74.5 2.4 %copy-start.3 = (bf16[4,13,13,128,32]{3,4,1,2,0:T(8,128)(2,1)}, bf16[4,13,13,128,32]{3,4,1,2,0:T(8,128)(2,1)S(1)}, u32[]{:S(2)}) copy-start(bf16[4,13,13,128,32]{3,4,1,2,0:T(8,128)(2,1)S(1)} %bitcast_dynamic-update-slice_fusion) | copy-start | bytes 16613380
Sparse Core Ops, SparseCore 0:
  79.5 21.0 all-gather.1
where the time goes:
time: 114 us; the launch traced here: 113 us
  waiting for transfers between devices  55.8 us (49%)
  local copies, waits for them, and re-layouts  24.5 us (21%)
  between operations  13.6 us (12%)
  matrix products  7.86 us (7%)
  starting transfers between devices  6.39 us (6%)
  other arithmetic  4.6 us (4%)
    all_to_all x1, waiting for transfers between devices, body(): lax.all_to_all(outgoing, 'rows', split_axis=0, concat_axis=0, tiled=True)  34.6 us
    all_gather x1, waiting for transfers between devices, body(): lax.all_gather(square, 'cols', axis=3, tiled=True)  21.2 us
    unnamed x22, local copies, waits for them, and re-layouts  9.24 us
    squeeze x6, local copies, waits for them, and re-layouts, body(): picked[:, slot_index, :slot_count - offset]  6.81 us
    all_to_all x1, starting transfers between devices, body(): lax.all_to_all(outgoing, 'rows', split_axis=0, concat_axis=0, tiled=True)  6.35 us
    dot_general x1, matrix products, body(): jnp.einsum('iapq,iasqc->ispc', lax.all_gather(square, 'cols', axis=3, til...  5.45 us
    gather x1, local copies, waits for them, and re-layouts, body(): picked = lookup[table_pick]  3.57 us
    dot_general x1, matrix products, body(): jnp.einsum('iapq,iasqc->ispc', full_rows, windows, preferred_element_type...  2.42 us
  transfers between devices with their start and end apart: 2, of which 2 were waited for; matrix products, arithmetic and copies ran while one was open for 1% of the time, Pallas kernels for 0%

commit v1 on v0

v1 whole, which is shorter than its diff:
```python
import functools

import jax
import jax.numpy as jnp
from jax import lax
from jax.experimental import pallas as pl
from jax.experimental.pallas import tpu as pltpu
from jax.sharding import PartitionSpec as P

CAP = 2
BAND = 16
CHUNKS = 3
MESH = pl.DeviceIdType.MESH


def kernel(
    owners, rows, slots, size, strip, band, most,
    cl, blocks, out,
    xt, send, tab, win, own, sq, gat, full,
    owner_of, first_code, first_weight, base_low, base_high, cum, source,
    send_sem, recv_sem, csend_sem, crecv_sem,
):
    middle = (slots - 1) // 2
    last = slots - 1
    count = rows * slots
    me = lax.axis_index("rows")
    part = lax.axis_index("cols")
    high, low = part // 2, part % 2
    sibling = high * 2 + (1 - low)
    across = (1 - high) * 2 + low
    far = (1 - high) * 2 + (1 - low)
    first = me * rows
    local_base = owners * band
    chunk = most // CHUNKS

    def peer_of(j):
        return lax.rem(me + owners // 2 + ((j + 1) // 2) * (1 - 2 * (j % 2)), owners)

    barrier = pltpu.get_barrier_semaphore()

    @pl.loop(0, owners - 1)
    def _(j):
        pl.semaphore_signal(barrier, inc=1, device_id={"rows": peer_of(j)}, device_id_type=MESH)

    for other in (sibling, across):
        pl.semaphore_signal(barrier, inc=1, device_id={"cols": other}, device_id_type=MESH)

    pick = (
        lax.broadcasted_iota(jnp.int32, (strip, size), 1)
        == lax.broadcasted_iota(jnp.int32, (strip, size), 0) + part * strip
    ).astype(jnp.bfloat16)
    zero_block = jnp.zeros((strip, size), jnp.bfloat16)
    xt[count] = zero_block
    sq[count] = zero_block
    for k in range(rows):
        for b in range(slots):
            n = k * slots + b
            column = cl[first + k, b]
            owner_of[n] = jnp.where(column >= 0, jnp.maximum(column, 0) // rows, -1)
            block = blocks[k, b]
            block = jnp.where(column >= 0, block, jnp.zeros_like(block))
            own[k, :, b * size : (b + 1) * size] = block
            strip_t = lax.dot_general(
                pick, block, (((1,), (1,)), ((), ())), preferred_element_type=jnp.float32
            ).astype(jnp.bfloat16)
            xt[n] = strip_t
            tab[local_base + n] = strip_t

    pl.semaphore_wait(barrier, owners - 1 + 2)

    def band_copy(src, dst_owner, peer):
        return pltpu.make_async_remote_copy(
            src_ref=send.at[src],
            dst_ref=tab.at[pl.ds(dst_owner * band, band)],
            send_sem=send_sem.at[src],
            recv_sem=recv_sem.at[dst_owner],
            device_id={"rows": peer},
            device_id_type=MESH,
        )

    @pl.loop(0, owners - 1)
    def _(j):
        peer = peer_of(j)
        lowest = jnp.int32(count)
        highest = jnp.int32(-1)
        for n in range(count):
            hit = owner_of[n] == peer
            lowest = jnp.minimum(lowest, jnp.where(hit, n, count))
            highest = jnp.maximum(highest, jnp.where(hit, n, -1))
        has_one = highest >= 0
        has_two = highest > lowest
        code0 = jnp.where(has_one, lowest, 0)
        code1 = jnp.where(has_two, highest, 0)
        row0, row1 = code0 // slots, code1 // slots
        slot0, slot1 = code0 - row0 * slots, code1 - row1 * slots
        weight0 = jnp.where(has_one, last - jnp.abs(slot0 - middle), 0)
        weight1 = jnp.where(has_two, last - jnp.abs(slot1 - middle), 0)
        start0 = jnp.maximum(slot0 - middle, 0)
        start1 = jnp.maximum(slot1 - middle, 0)
        for u in range(band):
            in0 = u < weight0
            in1 = u < weight0 + weight1
            place = jnp.where(in0, start0 + u, start1 + u - weight0)
            skip = jnp.where(in0, slot0, slot1)
            place = place + jnp.where(place >= skip, 1, 0)
            entry = jnp.where(in0, row0, row1) * slots + place
            entry = jnp.where(in1, entry, count)
            send[peer, u] = xt[entry]
        band_copy(peer, me, peer).start()
        key0 = cl[first + row0, slot0] * slots + last - slot0
        key1 = cl[first + row1, slot1] * slots + last - slot1
        swap = has_two & (key1 < key0)
        first_code[peer] = jnp.where(swap, code1, code0)
        first_weight[peer] = jnp.where(swap, weight1, weight0)

    first_code[me] = 0
    first_weight[me] = 0

    running = jnp.int32(0)
    for i in range(rows):
        for a in range(slots):
            n = i * slots + a
            column = cl[first + i, a]
            running = running + jnp.where(column >= 0, 1, 0)
            cum[n] = running
            column = jnp.where(column >= 0, column, first + i)
            owner = column // rows
            local = owner == me
            begin = max(0, middle - a)
            remote = owner * band + jnp.where(first_code[owner] == n, 0, first_weight[owner])
            here = local_base + (column - first) * slots + begin
            base_low[n] = jnp.where(local, here, remote)
            base_high[n] = jnp.where(local, here + 1, remote)

    @pl.loop(0, most)
    def _(t):
        entry = jnp.int32(0)
        for n in range(count):
            entry = entry + jnp.where(cum[n] <= t, 1, 0)
        source[t] = entry

    @pl.loop(0, rows)
    def _(i):
        for a in range(slots):
            lanes = slice(a * size, (a + 1) * size)
            for s in range(slots):
                b = s - a + middle
                span = slice(s * strip, (s + 1) * strip)
                if b < 0 or b >= slots:
                    win[i, span, lanes] = zero_block
                elif a == middle:
                    win[i, span, lanes] = xt[i * slots + s]
                elif s == middle:
                    win[i, span, lanes] = own[i, pl.ds(pl.multiple_of(part * strip, strip), strip), lanes]

    @pl.loop(0, owners - 1)
    def _(j):
        peer = peer_of(j)
        band_copy(peer, peer, peer).wait_recv()

    @pl.loop(0, rows)
    def _(i):
        for a in range(slots):
            if a == middle:
                continue
            n = i * slots + a
            low_at, high_at = base_low[n], base_high[n]
            begin = max(0, middle - a)
            for s in range(slots):
                b = s - a + middle
                if b < 0 or b >= slots or s == middle:
                    continue
                if s < middle:
                    entry = low_at + (b - begin)
                else:
                    entry = high_at + (b - begin - 1)
                win[i, s * strip : (s + 1) * strip, a * size : (a + 1) * size] = tab[entry]
        total = lax.dot_general(
            win[i], own[i], (((1,), (1,)), ((), ())), preferred_element_type=jnp.float32
        )
        for s in range(slots):
            value = total[s * strip : (s + 1) * strip]
            value = jnp.where(cl[first + i, s] >= 0, value, 0.0)
            sq[i * slots + s] = value.astype(jnp.bfloat16)

    def strip_copy(which, piece, peer, sem):
        span = pl.ds(piece * chunk, chunk)
        return pltpu.make_async_remote_copy(
            src_ref=gat.at[which, span],
            dst_ref=gat.at[which, span],
            send_sem=csend_sem.at[sem, piece],
            recv_sem=crecv_sem.at[sem, piece],
            device_id={"cols": peer},
            device_id_type=MESH,
        )

    for piece in range(CHUNKS):
        for t in range(piece * chunk, (piece + 1) * chunk):
            gat[part, t] = sq[source[t]]
        strip_copy(part, piece, across, 0).start()
        strip_copy(part, piece, sibling, 1).start()
    for piece in range(CHUNKS):
        strip_copy(across, piece, across, 0).wait_recv()
        strip_copy(across, piece, sibling, 2).start()
    for piece in range(CHUNKS):
        strip_copy(sibling, piece, sibling, 1).wait_recv()
    for piece in range(CHUNKS):
        strip_copy(far, piece, sibling, 2).wait_recv()

    @pl.loop(0, rows)
    def _(i):
        for a in range(slots):
            n = i * slots + a
            present = cl[first + i, a] >= 0
            entry = jnp.minimum(jnp.maximum(cum[n] - 1, 0), most - 1)
            for c in range(size // strip):
                value = gat[c, entry]
                value = jnp.where(present, value, jnp.zeros_like(value))
                full[a * size + c * strip : a * size + (c + 1) * strip, :] = value
        total = jnp.dot(win[i], full[...], preferred_element_type=jnp.float32)
        for s in range(slots):
            value = 3.0 * sq[i * slots + s].astype(jnp.float32) - 2.0 * total[s * strip : (s + 1) * strip]
            value = jnp.where(cl[first + i, s] >= 0, value, 0.0)
            out[i, s] = value.astype(jnp.bfloat16)

    @pl.loop(0, owners - 1)
    def _(j):
        peer = peer_of(j)
        band_copy(peer, me, peer).wait_send()

    for piece in range(CHUNKS):
        strip_copy(part, piece, across, 0).wait_send()
        strip_copy(part, piece, sibling, 1).wait_send()
        strip_copy(across, piece, sibling, 2).wait_send()


def body(column_lists, block_values):
    rows, slots, size, _ = block_values.shape
    owners = lax.axis_size("rows")
    parts = lax.axis_size("cols")
    assert parts == 4
    strip = size // parts
    band = BAND - CAP
    count = rows * slots
    most = min(count, rows * rows + CAP * (owners - 1))
    most = -(-most // CHUNKS) * CHUNKS
    bf16 = jnp.bfloat16
    result = pl.pallas_call(
        functools.partial(kernel, owners, rows, slots, size, strip, band, most),
        out_shape=jax.ShapeDtypeStruct((rows, slots, strip, size), bf16),
        in_specs=[
            pl.BlockSpec(memory_space=pltpu.SMEM),
            pl.BlockSpec(memory_space=pltpu.VMEM),
        ],
        out_specs=pl.BlockSpec(memory_space=pltpu.VMEM),
        scratch_shapes=[
            pltpu.VMEM((count + 1, strip, size), bf16),
            pltpu.VMEM((owners, band, strip, size), bf16),
            pltpu.VMEM((owners * band + count, strip, size), bf16),
            pltpu.VMEM((rows, slots * strip, slots * size), bf16),
            pltpu.VMEM((rows, size, slots * size), bf16),
            pltpu.VMEM((count + 1, strip, size), bf16),
            pltpu.VMEM((parts, most, strip, size), bf16),
            pltpu.VMEM((slots * size, size), bf16),
            pltpu.SMEM((count,), jnp.int32),
            pltpu.SMEM((owners,), jnp.int32),
            pltpu.SMEM((owners,), jnp.int32),
            pltpu.SMEM((count,), jnp.int32),
            pltpu.SMEM((count,), jnp.int32),
            pltpu.SMEM((count,), jnp.int32),
            pltpu.SMEM((most,), jnp.int32),
            pltpu.SemaphoreType.DMA((owners,)),
            pltpu.SemaphoreType.DMA((owners,)),
            pltpu.SemaphoreType.DMA((3, CHUNKS)),
            pltpu.SemaphoreType.DMA((3, CHUNKS)),
        ],
        compiler_params=pltpu.CompilerParams(
            collective_id=0, has_side_effects=True, vmem_limit_bytes=48 * 1024 * 1024
        ),
    )(column_lists, block_values)
    return jnp.swapaxes(result, 2, 3)


def solution(mesh):
    in_specs = (P(), P("rows", None, None, None))
    out_specs = P("rows", None, None, "cols")
    return jax.shard_map(body, mesh=mesh, in_specs=in_specs, out_specs=out_specs, check_vma=False)
```

time: 114 us -> 42.2 us (0.37)
  the two profiles are of different devices: /device:TPU:1 before, /device:TPU:11 now
where the time goes in v1:
time: 42.2 us; the launch traced here: 42 us
  Pallas kernels  39 us (92%)
  local copies, waits for them, and re-layouts  2.99 us (7%)
    pallas_call x1, Pallas kernels, body(): pl.pallas_call(functools.partial(kernel, owners, rows, slots, size, strip...  39 us
    unnamed x4, local copies, waits for them, and re-layouts  2.99 us

profile of v1, /device:TPU:11, one launch (start us, length us, event | category | flops | bytes accessed | tf_op | source)
XLA Modules:
  0.0 42.0 jit_solution(14985294091317931394)
XLA Ops:
  0.0 0.8 %copy.3.cl = s32[32,13]{1,0:T(8,128)S(1)} copy(s32[32,13]{0,1:T(8,128)} %param.2) | data formatting | bytes 3328 | tf_op args[0]
  0.8 0.0 copy-start
  0.8 1.5 %copy-done = bf16[4,13,128,128]{3,2,1,0:T(8,128)(2,1)S(1)} copy-done((bf16[4,13,128,128]{3,2,1,0:T(8,128)(2,1)S(1)}, bf16[4,13,128,128]{3,2,1,0:T(8,128)(2,1)}, u32[]{:S(2)}) %copy-start) | copy-done | bytes 1703960
  2.2 39.0 %shard_map.28 = bf16[4,13,32,128]{3,2,1,0:T(8,128)(2,1)S(1)} custom-call(s32[32,13]{1,0:T(8,128)S(1)} %copy.3.cl, bf16[4,13,128,128]{3,2,1,0:T(8,128)(2,1)S(1)} %copy-done), custom_call_target="tpu_custom_call" | custom-call | tf_op jit(solution)/shard_map/pallas_call | solution.py:248
  41.3 0.8 %copy.5 = bf16[4,13,128,32]{2,3,1,0:T(8,128)(2,1)} copy(bf16[4,13,128,32]{2,3,1,0:T(8,128)(2,1)S(1)} %bitcast.1) | data formatting | bytes 851968
Async XLA Ops:
  0.8 1.5 %copy-start = (bf16[4,13,128,128]{3,2,1,0:T(8,128)(2,1)S(1)}, bf16[4,13,128,128]{3,2,1,0:T(8,128)(2,1)}, u32[]{:S(2)}) copy-start(bf16[4,13,128,128]{3,2,1,0:T(8,128)(2,1)} %blocks.1) | copy-start | bytes 5111812
